TPU v7x, 32 devices: a whole 2x2x4 slice. The times are simulated.
32 devices in a mesh: gx: 4 (over y, core), gy: 8 (over z, x).
Axes of the slice: x: 2, y: 2, z: 4, core: 2. Of those that a mesh axis runs over, the one named last changes fastest.
Arguments:
- raw_window: float32 [2048, 16384], P('gx', 'gy'), may hold values from -6 to 6
- source_ids: int32 [256], P(('gx', 'gy')), may hold values from 0 to 2047, as said below
- pair_source: int32 [4096], P(('gx', 'gy')), may hold values from 0 to 255
- pair_holder: int32 [4096, 1], P(('gx', 'gy')), may hold values from 0 to 31; in each aligned block of 128 rows (0 to 127, 128 to 255, ...) at most 8 rows name the same one
- pair_receiver: int32 [4096], P(('gx', 'gy')), may hold values from 0 to 63
Outputs:
- correlations: float32 [4096, 512], P(('gx', 'gy'))
Inputs may be any that keep to these rules, and one draw needn't show every extreme that they name: The ids are distinct, and source k is a channel of the device that holds channels from (k // 8) * 64 on: source_ids[k] // 64 == k // 8. `pair_holder`: among the 128 pairs of one device, at most 8 name the same holder, a bound that some block reaches; every device is named by some pair.
All inputs are finite; a program needn't handle non-finite values.
Results may differ from a plain program's by a relative error of at most 0.0095.
Values may be sent and summed in bfloat16 or wider, within the bound.
A program may use at most 128 MiB of HBM per device.

v0:
```python
import math

import jax
import jax.numpy as jnp
from jax import lax
from jax.sharding import PartitionSpec as P

NBIN = 2048
SEGLEN = 4096
NSEG = 4
BAND = 64
NLAG = 512


def split_table(table):
    upper = table.astype(jnp.bfloat16)
    lower = (table - upper.astype(jnp.float32)).astype(jnp.bfloat16)
    return (upper, lower)


def inverse_table():
    bins = jnp.arange(NBIN, dtype=jnp.int32)
    lags = (jnp.arange(NLAG, dtype=jnp.int32) - NLAG // 2) % SEGLEN
    phase = bins[:, None] * lags[None, :] % SEGLEN
    angle = phase.astype(jnp.float32) * (2.0 * math.pi / SEGLEN)
    weight = jnp.where(bins == 0, 1.0, 2.0).astype(jnp.float32) * (0.5 / math.sqrt(NSEG * NBIN))
    return jnp.concatenate(
        [weight[:, None] * jnp.cos(angle), -weight[:, None] * jnp.sin(angle)], axis=0
    )


def whiten_block(seg_rows, block, width):
    times = jnp.arange(SEGLEN, dtype=jnp.int32)
    bins = block * width + jnp.arange(width, dtype=jnp.int32)
    phase = times[:, None] * bins[None, :] % SEGLEN
    angle = phase.astype(jnp.float32) * (2.0 * math.pi / SEGLEN)
    upper, lower = split_table(jnp.concatenate([jnp.cos(angle), -jnp.sin(angle)], axis=1))
    spectrum = jnp.dot(seg_rows, upper, preferred_element_type=jnp.float32)
    spectrum = spectrum + jnp.dot(seg_rows, lower, preferred_element_type=jnp.float32)
    real_part = spectrum[:, :width]
    imag_part = spectrum[:, width:]
    count = seg_rows.shape[0]
    power = (real_part * real_part + imag_part * imag_part).reshape(count, width // BAND, BAND)
    level = jnp.repeat(jnp.sqrt(jnp.mean(power, axis=2) + 1e-06), BAND, axis=1)
    return jnp.stack([real_part / level, imag_part / level], axis=1).astype(jnp.bfloat16)


def correlate(source_rows, receiver_rows, upper, lower):
    first = source_rows.astype(jnp.float32)
    second = receiver_rows.astype(jnp.float32)
    real_part = jnp.sum(first[:, :, 0] * second[:, :, 0] + first[:, :, 1] * second[:, :, 1], axis=1)
    imag_part = jnp.sum(first[:, :, 1] * second[:, :, 0] - first[:, :, 0] * second[:, :, 1], axis=1)
    cross = jnp.concatenate([real_part, imag_part], axis=1).astype(jnp.bfloat16)
    result = jnp.dot(cross, upper, preferred_element_type=jnp.float32)
    return result + jnp.dot(cross, lower, preferred_element_type=jnp.float32)


def body(raw_window, source_ids, pair_source, pair_holder, pair_receiver):
    groups = lax.axis_size("gy")
    devices = lax.axis_size("gx") * groups
    span = raw_window.shape[1]
    sample = (lax.axis_index("gy") * span + jnp.arange(span, dtype=jnp.int32)) % SEGLEN
    taper = jnp.sin(math.pi * (sample.astype(jnp.float32) + 0.5) / SEGLEN) ** 2
    tapered = (raw_window * taper[None, :]).astype(jnp.bfloat16)
    regrouped = lax.all_to_all(tapered, "gy", split_axis=0, concat_axis=1, tiled=True)
    channels = regrouped.shape[0]
    seg_rows = regrouped.reshape(channels * NSEG, SEGLEN)
    width = min(256, NBIN)

    def one_block(block):
        return whiten_block(seg_rows, block, width)

    blocks = lax.map(one_block, jnp.arange(NBIN // width, dtype=jnp.int32))
    whitened = jnp.transpose(blocks, (1, 2, 0, 3)).reshape(channels, NSEG, 2, NBIN)
    here = lax.axis_index("gx") * groups + lax.axis_index("gy")
    mine = jnp.take(whitened, source_ids - here * channels, axis=0)
    sources = lax.all_gather(mine, ("gx", "gy"), axis=0, tiled=True)
    pairs = pair_source.shape[0]
    slots = 2 * pairs // devices
    holder = pair_holder[:, 0]
    onehot = (holder[:, None] == jnp.arange(devices, dtype=jnp.int32)[None, :]).astype(jnp.int32)
    earlier = jnp.cumsum(onehot, axis=0) - onehot
    rank = jnp.sum(earlier * onehot, axis=1)
    slot = holder * slots + rank
    wanted = jnp.stack([pair_receiver, pair_source], axis=1)
    outgoing = jnp.full((devices * slots, 2), -1, jnp.int32).at[slot].set(wanted)
    incoming = lax.all_to_all(outgoing, ("gx", "gy"), split_axis=0, concat_axis=0, tiled=True)
    asked_receiver = jnp.clip(incoming[:, 0], 0, channels - 1)
    upper, lower = split_table(inverse_table())
    asked_source = jnp.clip(incoming[:, 1], 0, sources.shape[0] - 1)
    computed = correlate(
        jnp.take(sources, asked_source, axis=0),
        jnp.take(whitened, asked_receiver, axis=0),
        upper,
        lower,
    )
    returned = lax.all_to_all(computed, ("gx", "gy"), split_axis=0, concat_axis=0, tiled=True)
    return jnp.take(returned, slot, axis=0)


def solution(mesh):
    return jax.shard_map(
        body,
        mesh=mesh,
        in_specs=(
            P("gx", "gy"),
            P(("gx", "gy")),
            P(("gx", "gy")),
            P(("gx", "gy"), None),
            P(("gx", "gy")),
        ),
        out_specs=P(("gx", "gy"), None),
        check_vma=False,
    )
```

profile of v0, /device:TPU:0, one launch (start us, length us, event | category | flops | bytes accessed | tf_op | source)
XLA Modules:
  0.0 415.3 jit_solution(16252934427860859862)
XLA Ops:
  6.6 4.0 multiply_convert_fusion
  10.6 7.3 %all-to-all-start.1 = ((bf16[8,64,2048]{2,1,0:T(8,128)(2,1)}), bf16[8,64,2048]{2,1,0:T(8,128)(2,1)S(1)}, u32[]{:S(2)}, u32[]{:S(2)}) async-start(bf16[8,64,2048]{2,1,0:T(8,128)(2,1)} %bitcast.60), calls=%async_computation.1 | async-start | bytes 4194304 | tf_op jit(solution)/shard_map/all_to_all | solution.py:65
  18.0 48.1 %all-to-all-done.1 = bf16[8,64,2048]{2,1,0:T(8,128)(2,1)S(1)} async-done(((bf16[8,64,2048]{2,1,0:T(8,128)(2,1)}), bf16[8,64,2048]{2,1,0:T(8,128)(2,1)S(1)}, u32[]{:S(2)}, u32[]{:S(2)}) %all-to-all-start.1) | async-done | bytes 2097184 | tf_op jit(solution)/shard_map/all_to_all | solution.py:65
  71.2 171.0 %while.12 = (s32[]{:T(128)}, bf16[8,256,2,256]{1,3,2,0:T(8,128)(2,1)}, s32[8]{0:T(128)S(1)}, bf16[256,4096]{1,0:T(8,128)(2,1)S(1)}, s32[]{:T(128)}, /*index=5*/s32[1]{0:T(128)}) while((s32[]{:T(128)}, bf16[8,256,2,256]{1,3,2,0:T(8,128)(2,1)}, s32[8]{0:T(128)S(1)}, bf16[256,4096]{1,0:T(8,128)(2,1)S(1)}, s32[]{:T(128)}, ...), condition=%wide.region_5.6_spmd, body=%wide.region_3.5_spmd.sunk | while | flops 2183267584 | bytes 32787040 | solution.py:73
  72.5 16.5 %fusion.59 = (f32[4096,256]{1,0:T(8,128)S(1)}, f32[4096,256]{1,0:T(8,128)S(1)}) fusion(s32[256]{0:T(256)S(1)} %iota_add_fusion.2), kind=kLoop, calls=%fused_computation.20.clone.1 | loop fusion | flops 15728640 | bytes 8389632 | tf_op jit(solution)/shard_map/while/body/eval_jaxpr/cos | solution.py:37
  93.9 16.5 %fusion.59 = (f32[4096,256]{1,0:T(8,128)S(1)}, f32[4096,256]{1,0:T(8,128)S(1)}) fusion(s32[256]{0:T(256)S(1)} %iota_add_fusion.2), kind=kLoop, calls=%fused_computation.20.clone.1 | loop fusion | flops 15728640 | bytes 8389632 | tf_op jit(solution)/shard_map/while/body/eval_jaxpr/cos | solution.py:37
  115.2 16.5 %fusion.59 = (f32[4096,256]{1,0:T(8,128)S(1)}, f32[4096,256]{1,0:T(8,128)S(1)}) fusion(s32[256]{0:T(256)S(1)} %iota_add_fusion.2), kind=kLoop, calls=%fused_computation.20.clone.1 | loop fusion | flops 15728640 | bytes 8389632 | tf_op jit(solution)/shard_map/while/body/eval_jaxpr/cos | solution.py:37
  136.6 16.5 %fusion.59 = (f32[4096,256]{1,0:T(8,128)S(1)}, f32[4096,256]{1,0:T(8,128)S(1)}) fusion(s32[256]{0:T(256)S(1)} %iota_add_fusion.2), kind=kLoop, calls=%fused_computation.20.clone.1 | loop fusion | flops 15728640 | bytes 8389632 | tf_op jit(solution)/shard_map/while/body/eval_jaxpr/cos | solution.py:37
  158.0 16.5 %fusion.59 = (f32[4096,256]{1,0:T(8,128)S(1)}, f32[4096,256]{1,0:T(8,128)S(1)}) fusion(s32[256]{0:T(256)S(1)} %iota_add_fusion.2), kind=kLoop, calls=%fused_computation.20.clone.1 | loop fusion | flops 15728640 | bytes 8389632 | tf_op jit(solution)/shard_map/while/body/eval_jaxpr/cos | solution.py:37
  179.3 16.5 %fusion.59 = (f32[4096,256]{1,0:T(8,128)S(1)}, f32[4096,256]{1,0:T(8,128)S(1)}) fusion(s32[256]{0:T(256)S(1)} %iota_add_fusion.2), kind=kLoop, calls=%fused_computation.20.clone.1 | loop fusion | flops 15728640 | bytes 8389632 | tf_op jit(solution)/shard_map/while/body/eval_jaxpr/cos | solution.py:37
  200.7 16.5 %fusion.59 = (f32[4096,256]{1,0:T(8,128)S(1)}, f32[4096,256]{1,0:T(8,128)S(1)}) fusion(s32[256]{0:T(256)S(1)} %iota_add_fusion.2), kind=kLoop, calls=%fused_computation.20.clone.1 | loop fusion | flops 15728640 | bytes 8389632 | tf_op jit(solution)/shard_map/while/body/eval_jaxpr/cos | solution.py:37
  222.1 16.5 %fusion.59 = (f32[4096,256]{1,0:T(8,128)S(1)}, f32[4096,256]{1,0:T(8,128)S(1)}) fusion(s32[256]{0:T(256)S(1)} %iota_add_fusion.2), kind=kLoop, calls=%fused_computation.20.clone.1 | loop fusion | flops 15728640 | bytes 8389632 | tf_op jit(solution)/shard_map/while/body/eval_jaxpr/cos | solution.py:37
  242.3 4.7 %copy.30 = bf16[256,2,8,256]{3,2,1,0:T(8,128)(2,1)} copy(bf16[256,2,8,256]{0,3,1,2:T(8,128)(2,1)} %bitcast.15) | data formatting | bytes 4194304 | tf_op jit(solution)/shard_map/transpose | solution.py:74
  254.2 3.7 all-to-all-start
  257.9 18.2 %cosine_multiply_fusion = (f32[2048,512]{1,0:T(8,128)}, f32[2048,512]{1,0:T(8,128)}) fusion(s32[512]{0:T(512)S(1)} %add_select_fusion.3, f32[2048]{0:T(1024)S(1)} %get-tuple-element.86, f32[2048]{0:T(1024)S(1)} %get-tuple-element.87), kind=kLoop, calls=%fused_computation.49 | loop fusion | flops 16777216 | bytes 8407040 | tf_op jit(solution)/shard_map/mul | solution.py:28
  279.2 12.7 %gather_fusion.2 = bf16[256,4,2,2048]{3,1,2,0:T(4,128)(2,1)} fusion(bf16[64,4,2,2048]{3,1,2,0:T(4,128)(2,1)S(1)} %copy.32, s32[1024]{0:T(1024)S(1)} %pad_clamp_fusion.1), kind=kCustom, calls=%fused_computation.2 | custom fusion | bytes 16778240 | tf_op jit(solution)/shard_map/jit(_take)/gather | solution.py:93
  291.9 9.9 %select_convert_fusion = f32[256,4,2,2048]{3,1,2,0:T(4,128)} fusion(bf16[256,4,2,2048]{3,1,2,0:T(4,128)(2,1)} %gather_fusion.2, pred[256]{0:T(512)(128)(4,1)S(1)} %get-tuple-element.82), kind=kLoop, calls=%fused_computation.38 | loop fusion | flops 8388608 | bytes 25166080 | tf_op jit(solution)/shard_map/convert_element_type | solution.py:50
  301.7 26.6 %all-gather.2.cloned.1.call-done = bf16[256,4,2,2048]{3,1,2,0:T(4,128)(2,1)} async-done(((bf16[8,4,2,2048]{3,1,2,0:T(4,128)(2,1)}), bf16[256,4,2,2048]{3,1,2,0:T(4,128)(2,1)}) %all-gather.2.cloned.1.call-update) | async-done | bytes 8388624 | tf_op jit(solution)/shard_map/all_gather | solution.py:77
  328.4 16.1 %gather_fusion.1 = bf16[256,4,2,2048]{3,1,2,0:T(4,128)(2,1)} fusion(bf16[256,4,2,2048]{3,1,2,0:T(4,128)(2,1)} %all-gather.2.cloned.1.call-done, s32[1024]{0:T(1024)S(1)} %pad_clamp_fusion.2), kind=kCustom, calls=%fused_computation.1 | custom fusion | bytes 16778240 | tf_op jit(solution)/shard_map/jit(_take)/gather | solution.py:92
  344.4 10.5 %select_convert_fusion.1 = f32[256,4,2,2048]{3,1,2,0:T(4,128)} fusion(bf16[256,4,2,2048]{3,1,2,0:T(4,128)(2,1)} %gather_fusion.1, pred[256]{0:T(512)(128)(4,1)S(1)} %get-tuple-element.72), kind=kLoop, calls=%fused_computation.39 | loop fusion | flops 8388608 | bytes 25166080 | tf_op jit(solution)/shard_map/convert_element_type | solution.py:49
  354.9 3.6 copy-done
  358.5 22.6 %add_reduce_fusion = (bf16[256,2048]{1,0:T(8,128)(2,1)S(1)}, bf16[256,2048]{1,0:T(8,128)(2,1)}) fusion(f32[256,4,2,2048]{3,1,2,0:T(4,128)S(1)} %copy-done, f32[256,4,2,2048]{3,1,2,0:T(4,128)} %select_convert_fusion.1), kind=kLoop, calls=%fused_computation.37 | loop fusion | flops 15728640 | bytes 35651584 | tf_op jit(solution)/shard_map/reduce_sum | solution.py:51
  381.2 3.9 fusion.18
  390.6 16.3 %all-to-all-done.2 = f32[32,8,512]{2,1,0:T(8,128)S(1)} async-done(((f32[32,8,512]{2,1,0:T(8,128)}), f32[32,8,512]{2,1,0:T(8,128)S(1)}, u32[]{:S(2)}, u32[]{:S(2)}) %all-to-all-start.2) | async-done | bytes 524320 | tf_op jit(solution)/shard_map/all_to_all | solution.py:97
  (116 shorter events, 55.9 us)
Async XLA Ops:
  6.6 11.3 %copy-start.6 = (s32[8]{0:T(128)S(1)}, s32[8]{0:T(128)}, u32[]{:S(2)}) copy-start(s32[8]{0:T(128)} %param.8) | copy-start | bytes 100
  10.6 55.5 %all-to-all-start.1 = ((bf16[8,64,2048]{2,1,0:T(8,128)(2,1)}), bf16[8,64,2048]{2,1,0:T(8,128)(2,1)S(1)}, u32[]{:S(2)}, u32[]{:S(2)}) async-start(bf16[8,64,2048]{2,1,0:T(8,128)(2,1)} %bitcast.60), calls=%async_computation.1 | async-start | bytes 4194304 | tf_op jit(solution)/shard_map/all_to_all | solution.py:65
  17.9 310.5 %all-gather.2.cloned.1.call-start = ((), (), s32[]{:S(2)}) async-start(), calls=%async_computation.3 | async-start | bytes 8650752 | tf_op jit(solution)/shard_map/all_gather | solution.py:77
  242.3 9.6 %copy-start.5 = (s32[128,1]{0,1:T(1,128)S(1)}, s32[128,1]{0,1:T(1,128)}, u32[]{:S(2)}) copy-start(s32[128,1]{0,1:T(1,128)} %param.10) | copy-start | bytes 1540
  242.3 9.8 %copy-start.7 = (s32[128]{0:T(128)S(1)}, s32[128]{0:T(128)}, u32[]{:S(2)}) copy-start(s32[128]{0:T(128)} %param.9) | copy-start | bytes 1540
  242.3 9.8 %copy-start.8 = (s32[128]{0:T(128)S(1)}, s32[128]{0:T(128)}, u32[]{:S(2)}) copy-start(s32[128]{0:T(128)} %param.11) | copy-start | bytes 1540
  249.6 26.5 %copy-start.1 = (bf16[64,4,2,2048]{3,2,1,0:T(2,128)(2,1)}, bf16[64,4,2,2048]{3,2,1,0:T(2,128)(2,1)S(1)}, u32[]{:S(2)}) copy-start(bf16[64,4,2,2048]{3,2,1,0:T(2,128)(2,1)S(1)} %reshape.142) | copy-start | bytes 6291460
  254.2 21.9 %all-to-all-start = ((s32[32,8,2]{1,2,0:T(2,128)}), s32[32,8,2]{1,2,0:T(2,128)S(1)}, u32[]{:S(2)}, u32[]{:S(2)}) async-start(s32[32,8,2]{1,2,0:T(2,128)} %copy.27), calls=%async_computation | async-start | bytes 65536 | tf_op jit(solution)/shard_map/all_to_all | solution.py:87
  344.4 14.1 %copy-start = (f32[256,4,2,2048]{3,1,2,0:T(4,128)S(1)}, f32[256,4,2,2048]{3,1,2,0:T(4,128)}, u32[]{:S(2)}) copy-start(f32[256,4,2,2048]{3,1,2,0:T(4,128)} %select_convert_fusion) | copy-start | bytes 50331652
  358.5 22.6 %copy-start.2 = (f32[2048,512]{1,0:T(8,128)S(1)}, f32[2048,512]{1,0:T(8,128)}, u32[]{:S(2)}) copy-start(f32[2048,512]{1,0:T(8,128)} %get-tuple-element.84) | copy-start | bytes 12582916
  381.2 3.9 copy-start.3
  381.2 4.0 copy-start.4
  387.3 19.7 %all-to-all-start.2 = ((f32[32,8,512]{2,1,0:T(8,128)}), f32[32,8,512]{2,1,0:T(8,128)S(1)}, u32[]{:S(2)}, u32[]{:S(2)}) async-start(f32[32,8,512]{2,1,0:T(8,128)} %fusion.28), calls=%async_computation.2 | async-start | bytes 1048576 | tf_op jit(solution)/shard_map/all_to_all | solution.py:97
Sparse Core Ops, SparseCore 0:
  251.9 76.3 all-gather.1
where the time goes:
time: 416 us; the launch traced here: 415 us
  other arithmetic  206 us (50%)
  waiting for transfers between devices  91.1 us (22%)
  local copies, waits for them, and re-layouts  57.2 us (14%)
  matrix products  28 us (7%)
  starting transfers between devices  14.3 us (3%)
  between operations  13.6 us (3%)
  loops' own time  5.44 us (1%)
    cos x8, other arithmetic, whiten_block(): jnp.cos(angle)  132 us
    all_to_all x1, waiting for transfers between devices, body(): lax.all_to_all(tapered, 'gy', split_axis=0, concat_axis=1, tiled=True)  48.1 us
    all_gather x1, waiting for transfers between devices, body(): sources = lax.all_gather(mine, ('gx', 'gy'), axis=0, tiled=True)  26.6 us
    reduce_sum x1, other arithmetic, correlate(): jnp.sum(first[:, :, 0] * second[:, :, 0] + first[:, :, 1] * second[:, :,...  22.6 us
    mul x1, other arithmetic, inverse_table(): weight[:, None] * jnp.cos(angle)  18.2 us
    all_to_all x1, waiting for transfers between devices, body(): lax.all_to_all(computed, ('gx', 'gy'), split_axis=0, concat_axis=0, tiled...  16.3 us
    gather x1, local copies, waits for them, and re-layouts, body(): jnp.take(sources, asked_source, axis=0)  16.1 us
    gather x1, local copies, waits for them, and re-layouts, body(): jnp.take(whitened, asked_receiver, axis=0)  12.7 us
  transfers between devices with their start and end apart: 4, of which 3 were waited for; matrix products, arithmetic and copies ran while one was open for 11% of the time, Pallas kernels for 0%

commit v1 on v0

v1 whole, which is shorter than its diff:
```python
import functools
import math

import jax
import jax.numpy as jnp
import ml_dtypes
import numpy as np
from jax import lax
from jax.experimental import pallas as pl
from jax.experimental.pallas import tpu as pltpu
from jax.sharding import Mesh, PartitionSpec as P

NBIN = 2048
SEGLEN = 4096
NSEG = 4
BAND = 64
NLAG = 512
HALF = SEGLEN // 2
STEPS = 4
BANDS = NBIN // BAND // STEPS
WIDE = NBIN // 2 // STEPS
COLS = 4 * WIDE
BF16 = ml_dtypes.bfloat16
EVERY = ("gx", "seg", "part")


def step_bins(step):
    col = np.arange(WIDE)
    even = BAND * (step * BANDS + col % BANDS) + 2 * (col // BANDS)
    return even, even + 1


@functools.lru_cache(None)
def forward_tables():
    times = np.arange(HALF)
    tables = []
    for parity in range(2):
        steps = []
        for step in range(STEPS):
            angle = (times[:, None] * step_bins(step)[parity][None, :] % SEGLEN) * (2.0 * math.pi / SEGLEN)
            steps.append(np.concatenate([np.cos(angle), -np.sin(angle)], axis=1))
        tables.append(np.stack(steps).astype(BF16))
    return tables


@functools.lru_cache(None)
def inverse_table():
    lags = (np.arange(NLAG) - NLAG // 2) % SEGLEN
    rows = []
    for step in range(STEPS):
        for bins in step_bins(step):
            angle = (bins[:, None] * lags[None, :] % SEGLEN) * (2.0 * math.pi / SEGLEN)
            weight = np.where(bins == 0, 1.0, 2.0)[:, None] * (0.5 / math.sqrt(NSEG * NBIN))
            rows += [weight * np.cos(angle), -weight * np.sin(angle)]
    return np.concatenate(rows, axis=0).astype(BF16)


def dot(a, b):
    return jnp.dot(a, b, preferred_element_type=jnp.float32)


def whiten_kernel(first_ref, second_ref, sign_ref, pick_ref, even_ref, odd_ref, white_ref, mine_ref, sums, diffs):
    @pl.when(pl.program_id(0) == 0)
    def _():
        first = first_ref[...].astype(jnp.float32)
        second = second_ref[...].astype(jnp.float32)
        sums[...] = (first + second).astype(jnp.bfloat16)
        diffs[...] = ((first - second) * sign_ref[0, 0]).astype(jnp.bfloat16)

    even = dot(sums[...], even_ref[0])
    odd = dot(diffs[...], odd_ref[0])
    power = even * even + odd * odd
    total = power[:, 0:128]
    for lane in range(128, 2 * WIDE, 128):
        total = total + power[:, lane:lane + 128]
    shift = 64
    while shift >= BANDS:
        total = total + pltpu.roll(total, shift, 1)
        shift //= 2
    scale = lax.rsqrt(total * (1.0 / BAND) + 1e-06)
    scale = jnp.concatenate([scale] * (2 * WIDE // 128), axis=1)
    white = jnp.concatenate([even * scale, odd * scale], axis=1).astype(jnp.bfloat16)
    white_ref[...] = white
    rows = white.shape[0]
    chosen = pick_ref[...] == lax.broadcasted_iota(jnp.int32, (pick_ref.shape[0], rows), 1)
    mine_ref[...] = dot(chosen.astype(jnp.bfloat16), white).astype(jnp.bfloat16)


def whiten(first, second, sign, pick):
    even, odd = forward_tables()
    rows, count = first.shape[0], pick.shape[0]
    whole = lambda shape: pl.BlockSpec(shape, lambda g: (0, 0))
    return pl.pallas_call(
        whiten_kernel,
        grid=(STEPS,),
        in_specs=[
            whole((rows, HALF)),
            whole((rows, HALF)),
            pl.BlockSpec(memory_space=pltpu.SMEM),
            whole((count, 1)),
            pl.BlockSpec((1, HALF, 2 * WIDE), lambda g: (g, 0, 0)),
            pl.BlockSpec((1, HALF, 2 * WIDE), lambda g: (g, 0, 0)),
        ],
        out_specs=[
            pl.BlockSpec((rows, COLS), lambda g: (0, g)),
            pl.BlockSpec((count, COLS), lambda g: (0, g)),
        ],
        out_shape=[
            jax.ShapeDtypeStruct((rows, STEPS * COLS), jnp.bfloat16),
            jax.ShapeDtypeStruct((count, STEPS * COLS), jnp.bfloat16),
        ],
        scratch_shapes=[pltpu.VMEM((rows, HALF), jnp.bfloat16), pltpu.VMEM((rows, HALF), jnp.bfloat16)],
        compiler_params=pltpu.CompilerParams(vmem_limit_bytes=40 * 1024 * 1024),
        name="whiten",
    )(first, second, sign, pick, jnp.asarray(even), jnp.asarray(odd))


def correlate_kernel(source_ref, receiver_ref, sources_ref, white_ref, table_ref, out_ref):
    tile = source_ref.shape[0]
    ids = lax.broadcasted_iota(jnp.int32, (tile, sources_ref.shape[0]), 1)
    rows = lax.broadcasted_iota(jnp.int32, (tile, white_ref.shape[0]), 1)
    source = (source_ref[...] == ids).astype(jnp.bfloat16)
    receiver = (receiver_ref[...] == rows).astype(jnp.bfloat16)
    total = jnp.zeros((tile, NLAG), jnp.float32)
    for step in range(2 * STEPS):
        columns = slice(step * 2 * WIDE, (step + 1) * 2 * WIDE)
        a = dot(source, sources_ref[:, columns])
        b = dot(receiver, white_ref[:, columns])
        ar, ai, br, bi = a[:, :WIDE], a[:, WIDE:], b[:, :WIDE], b[:, WIDE:]
        cross = jnp.concatenate([ar * br + ai * bi, ai * br - ar * bi], axis=1).astype(jnp.bfloat16)
        total = total + dot(cross, table_ref[columns, :])
    out_ref[...] = total.astype(jnp.bfloat16)


def correlate(source, receiver, sources, white):
    slots = source.shape[0]
    tile = math.gcd(slots, 256)
    whole = lambda shape: pl.BlockSpec(shape, lambda g: (0, 0))
    return pl.pallas_call(
        correlate_kernel,
        grid=(slots // tile,),
        in_specs=[
            pl.BlockSpec((tile, 1), lambda g: (g, 0)),
            pl.BlockSpec((tile, 1), lambda g: (g, 0)),
            whole(sources.shape),
            whole(white.shape),
            whole((2 * NBIN, NLAG)),
        ],
        out_specs=pl.BlockSpec((tile, NLAG), lambda g: (g, 0)),
        out_shape=jax.ShapeDtypeStruct((slots, NLAG), jnp.bfloat16),
        compiler_params=pltpu.CompilerParams(vmem_limit_bytes=40 * 1024 * 1024),
        name="correlate",
    )(source, receiver, sources, white, jnp.asarray(inverse_table()))


def body(raw_window, source_ids, pair_source, pair_holder, pair_receiver):
    gx, seg, part = (lax.axis_index(name) for name in EVERY)
    parts = lax.axis_size("part")
    groups = NSEG * parts
    devices = lax.axis_size("gx") * groups
    channels, span = raw_window.shape
    rows = channels // parts
    block = channels // groups
    pairs = pair_source.shape[0]
    slots = 2 * pairs // devices

    holder = pair_holder[:, 0]
    order = jnp.arange(pairs, dtype=jnp.int32)
    same = (holder[:, None] == holder[None, :]) & (order[None, :] < order[:, None])
    slot = holder * slots + jnp.sum(same.astype(jnp.int32), axis=1)
    wanted = jnp.stack([pair_source, holder % NSEG * block + pair_receiver], axis=0)
    spots = jnp.arange(devices * slots, dtype=jnp.int32)
    match = slot[None, :] == spots[:, None]
    outgoing = jnp.max(jnp.where(match[None], wanted[:, None, :], -1), axis=2)
    packed = jnp.concatenate([outgoing.reshape(-1), source_ids])
    asked = lax.all_gather(packed, EVERY, axis=0)
    near = NSEG * slots
    start = (gx * parts + part) * near
    requests = asked[:, :2 * devices * slots].reshape(devices, 2, devices * slots)
    requests = lax.dynamic_slice_in_dim(requests, start, near, axis=2)
    asked_source = requests[:, 0].reshape(devices * near, 1)
    asked_receiver = requests[:, 1].reshape(devices * near, 1)
    picks = asked[:, 2 * devices * slots:]
    picks = lax.dynamic_slice_in_dim(picks, (gx * parts + part) * NSEG, NSEG, axis=0)
    pick = picks.reshape(-1, 1) - gx * channels - part * rows

    samples = part * span + jnp.arange(span, dtype=jnp.int32)
    taper = jnp.sin(math.pi * (samples.astype(jnp.float32) + 0.5) / SEGLEN) ** 2
    tapered = (raw_window * taper[None, :]).astype(jnp.bfloat16)
    if parts == 2:
        first = lax.dynamic_slice_in_dim(tapered, part * rows, rows, axis=0)
        away = lax.dynamic_slice_in_dim(tapered, (1 - part) * rows, rows, axis=0)
        second = lax.ppermute(away, "part", [(0, 1), (1, 0)])
        sign = jnp.where(part == 0, 1.0, -1.0).astype(jnp.float32).reshape(1, 1)
    else:
        segment = lax.all_to_all(tapered, "part", split_axis=0, concat_axis=1, tiled=True)
        first, second = segment[:, :HALF], segment[:, HALF:]
        sign = jnp.ones((1, 1), jnp.float32)
    white, mine = whiten(first, second, sign, pick)
    sources = lax.all_gather(mine, ("gx", "part"), axis=0, tiled=True)
    partial = correlate(asked_source, asked_receiver, sources, white)
    returned = lax.all_to_all(partial, EVERY, split_axis=0, concat_axis=0, tiled=True)

    keys = spots.reshape(devices // groups, 1, parts, near)
    keys = jnp.broadcast_to(keys, (devices // groups, NSEG, parts, near)).reshape(-1)
    chosen = (slot[:, None] == keys[None, :]).astype(jnp.bfloat16)
    return dot(chosen, returned)


def solution(mesh):
    n_gx, n_gy = mesh.devices.shape
    fine = Mesh(mesh.devices.reshape(n_gx, NSEG, n_gy // NSEG), EVERY)
    whole = P(EVERY)
    return jax.shard_map(
        body,
        mesh=fine,
        in_specs=(P("gx", ("seg", "part")), whole, whole, P(EVERY, None), whole),
        out_specs=P(EVERY, None),
        check_vma=False,
    )
```

time: 416 us -> 237 us (0.57)
  other arithmetic: 206 us -> 3.26 us
  waiting for transfers between devices: 91.1 us -> 176 us
  local copies, waits for them, and re-layouts: 57.2 us -> 12.7 us
  matrix products: 28 us -> 1.05 us
  Pallas kernels: 0 us -> 22.3 us
  starting transfers between devices: 14.3 us -> 7.65 us
  loops' own time: 5.44 us -> 0 us
    cos x8 -> x0, other arithmetic: 132 us -> none  [whiten_block(): jnp.cos(angle)]
    unnamed x1 -> x3, waiting for transfers between devices: 0.02 us -> 120 us
    all_to_all x3 -> x1, waiting for transfers between devices: 64.5 us -> 27.5 us  [body(): lax.all_to_all(partial, EVERY, split_axis=0, concat_axis=0, tiled=True)]
    gather x4 -> x0, local copies, waits for them, and re-layouts: 30.6 us -> none  [the longest x1 16.1 us: body(): jnp.take(sources, asked_source, axis=0)]
    dot_general x18 -> x1, matrix products: 28 us -> 1.05 us  [dot(): return jnp.dot(a, b, preferred_element_type=jnp.float32)]
    reduce_sum x10 -> x1, other arithmetic: 23.2 us -> 0.17 us  [body(): slot = holder * slots + jnp.sum(same.astype(jnp.int32), axis=1)]
    pallas_call x0 -> x2, Pallas kernels: none -> 22.3 us  [the longest x1 12.6 us: correlate(): pl.pallas_call(correlate_kernel, grid=(slots // tile,), in_specs=[pl.Bloc...]
    convert_element_type x3 -> x0, other arithmetic: 20.5 us -> none  [the longest x1 10.5 us: correlate(): first = source_rows.astype(jnp.float32)]
  transfers between devices with their start and end apart: 4 -> 4, of which waited for: 3 -> 3; matrix products, arithmetic and copies ran while one was open for 11% -> 1% of each run, Pallas kernels for 0% -> 0%
where the time goes in v1:
time: 237 us
  waiting for transfers between devices  176 us (74%)
  Pallas kernels  22.3 us (9%)
  between operations  13.6 us (6%)
  local copies, waits for them, and re-layouts  12.7 us (5%)
  starting transfers between devices  7.65 us (3%)
  other arithmetic  3.26 us (1%)
    unnamed x3, waiting for transfers between devices  120 us
    all_gather x1, waiting for transfers between devices, body(): sources = lax.all_gather(mine, ('gx', 'part'), axis=0, tiled=True)  29 us
    all_to_all x1, waiting for transfers between devices, body(): lax.all_to_all(partial, EVERY, split_axis=0, concat_axis=0, tiled=True)  27.5 us
    pallas_call x1, Pallas kernels, correlate(): pl.pallas_call(correlate_kernel, grid=(slots // tile,), in_specs=[pl.Bloc...  12.6 us
    unnamed x22, local copies, waits for them, and re-layouts  10 us
    pallas_call x1, Pallas kernels, whiten(): pl.pallas_call(whiten_kernel, grid=(STEPS,), in_specs=[whole((rows, HALF)...  9.74 us
  transfers between devices with their start and end apart: 4, of which 3 were waited for; matrix products, arithmetic and copies ran while one was open for 1% of the time, Pallas kernels for 0%

profile of v1, /device:TPU:0, one launch (start us, length us, event | category | flops | bytes accessed | tf_op | source)
XLA Modules:
  0.0 236.8 jit_solution(6578915721213133776)
XLA Ops:
  6.6 2.7 %multiply_convert_fusion = bf16[512,2048]{1,0:T(8,128)(2,1)S(1)} fusion(f32[512,2048]{1,0:T(8,128)} %param.8, f32[2048]{0:T(1024)S(1)} %sine_multiply_fusion), kind=kLoop, calls=%fused_computation | loop fusion | flops 2097152 | bytes 6299648 | tf_op jit(solution)/shard_map/convert_element_type | solution.py:189
  9.3 0.2 constant_dynamic-slice_fusion.1
  9.6 3.0 %collective-permute-start = (bf16[256,2048]{1,0:T(8,128)(2,1)S(1)}, bf16[256,2048]{1,0:T(8,128)(2,1)S(1)}, u32[]{:S(2)}, u32[]{:S(2)}) collective-permute-start(bf16[256,2048]{1,0:T(8,128)(2,1)S(1)} %get-tuple-element.9), channel_id=1, source_target_pairs={{0,1},{1,0},{2,3},{3,2},{4,5},{5,4},{6,7},{7,6},{8,9},{9,8},{10,11... | collective-permute-start | bytes 3145736 | tf_op jit(solution)/shard_map/ppermute | solution.py:193
  12.6 0.2 convert_reduce_fusion
  12.9 0.1 select_reduce_fusion
  13.1 0.1 add_dynamic-update-slice_fusion
  13.2 0.6 copy-done.5
  13.9 119.7 %all-reduce.3.cloned.1.call-done = s32[16640]{0:T(1024)} async-done(((s32[16640]{0:T(1024)}), s32[16640]{0:T(1024)}) %all-reduce.3.cloned.1.call-update) | async-done | bytes 66576
  133.6 1.0 reshape.115
  134.7 1.0 copy-done.3
  135.7 3.4 %copy-done = bf16[4,2048,512]{2,1,0:T(8,128)(2,1)S(1)} copy-done((bf16[4,2048,512]{2,1,0:T(8,128)(2,1)S(1)}, bf16[4,2048,512]{2,1,0:T(8,128)(2,1)}, u32[]{:S(2)}) %copy-start) | copy-done | bytes 8388632
  139.1 1.2 copy-done.4
  140.3 9.7 %whiten.1 = (bf16[256,4096]{1,0:T(8,128)(2,1)S(1)}, bf16[32,4096]{1,0:T(8,128)(2,1)}) custom-call(bf16[256,2048]{1,0:T(8,128)(2,1)S(1)} %get-tuple-element.10.first_ref, bf16[256,2048]{1,0:T(8,128)(2,1)S(1)} %copy-done.4, f32[1,1]{1,0:T(1,128)} %bitcast.5.sign_ref, s32[32,1]{1,0:T(8,128)S(1)} %sub.32.pick_ref, bf16[4,2048,512]{2,1,0:T(8,128)(2,1)S(1)} %copy-done, ...), custom_call_target="tpu_custom_call" | custom-call | tf_op jit(solution)/shard_map/whiten/pallas_call | solution.py:93
  150.1 0.1 constant_dynamic-slice_fusion.3
  150.3 0.5 reshape_squeeze.8.source_ref
  150.8 0.5 reshape_squeeze.9.receiver_ref
  151.3 29.0 %all-gather.3.cloned.1.call-done.sources_ref = bf16[256,4096]{1,0:T(8,128)(2,1)} async-done(((bf16[32,4096]{1,0:T(8,128)(2,1)}), bf16[256,4096]{1,0:T(8,128)(2,1)}) %all-gather.3.cloned.1.call-update) | async-done | bytes 2097168 | tf_op jit(solution)/shard_map/all_gather | solution.py:200
  180.4 2.2 copy-done.1
  182.5 1.6 copy-done.2
  184.1 12.6 %correlate.1 = bf16[1024,512]{1,0:T(8,128)(2,1)} custom-call(s32[1024,1]{1,0:T(8,128)S(1)} %reshape_squeeze.8.source_ref, s32[1024,1]{1,0:T(8,128)S(1)} %reshape_squeeze.9.receiver_ref, bf16[256,4096]{1,0:T(8,128)(2,1)S(1)} %copy-done.2, bf16[256,4096]{1,0:T(8,128)(2,1)S(1)} %get-tuple-element.8.white_ref, bf16[4096,512]{1,0:T(8,128)(2,1)S(1)} %copy-done.1), custom_call_target="tpu_custom_call" | custom-call | tf_op jit(solution)/shard_map/correlate/pallas_call | solution.py:139
  196.7 4.6 %all-to-all-start = ((bf16[32,32,512]{2,1,0:T(8,128)(2,1)}), bf16[32,32,512]{2,1,0:T(8,128)(2,1)S(1)}, u32[]{:S(2)}, u32[]{:S(2)}) async-start(bf16[32,32,512]{2,1,0:T(8,128)(2,1)} %bitcast.6), calls=%async_computation | async-start | bytes 2097152 | tf_op jit(solution)/shard_map/all_to_all | solution.py:202
  201.3 0.1 eq.60
  201.4 27.5 %all-to-all-done = bf16[32,32,512]{2,1,0:T(8,128)(2,1)S(1)} async-done(((bf16[32,32,512]{2,1,0:T(8,128)(2,1)}), bf16[32,32,512]{2,1,0:T(8,128)(2,1)S(1)}, u32[]{:S(2)}, u32[]{:S(2)}) %all-to-all-start) | async-done | bytes 1048608 | tf_op jit(solution)/shard_map/all_to_all | solution.py:202
  228.9 1.1 fusion
  (33 shorter events, 0.4 us)
Async XLA Ops:
  6.5 127.0 %all-reduce.3.cloned.1.call-start = ((), (), s32[]{:S(2)}) async-start(), calls=%async_computation.2 | async-start | bytes 139264
  6.6 6.0 %copy-start.8 = (s32[128,1]{0,1:T(1,128)S(1)}, s32[128,1]{0,1:T(1,128)}, u32[]{:S(2)}) copy-start(s32[128,1]{0,1:T(1,128)} %param.11) | copy-start | bytes 1540
  6.6 6.2 %copy-start.7 = (s32[128]{0:T(128)S(1)}, s32[128]{0:T(128)}, u32[]{:S(2)}) copy-start(s32[128]{0:T(128)} %param.12) | copy-start | bytes 1540
  6.6 6.2 %copy-start.9 = (s32[128]{0:T(128)S(1)}, s32[128]{0:T(128)}, u32[]{:S(2)}) copy-start(s32[128]{0:T(128)} %param.10) | copy-start | bytes 1540
  6.6 6.4 %copy-start.6 = (s32[8]{0:T(128)S(1)}, s32[8]{0:T(128)}, u32[]{:S(2)}) copy-start(s32[8]{0:T(128)} %param.9) | copy-start | bytes 100
  9.6 125.1 %collective-permute-start = (bf16[256,2048]{1,0:T(8,128)(2,1)S(1)}, bf16[256,2048]{1,0:T(8,128)(2,1)S(1)}, u32[]{:S(2)}, u32[]{:S(2)}) collective-permute-start(bf16[256,2048]{1,0:T(8,128)(2,1)S(1)} %get-tuple-element.9), channel_id=1, source_target_pairs={{0,1},{1,0},{2,3},{3,2},{4,5},{5,4},{6,7},{7,6},{8,9},{9,8},{10,11... | collective-permute-start | bytes 3145736 | tf_op jit(solution)/shard_map/ppermute | solution.py:193
  13.2 0.6 copy-start.5
  13.8 166.5 %all-gather.3.cloned.1.call-start = ((), (), s32[]{:S(2)}) async-start(), calls=%async_computation.1 | async-start | bytes 2359296 | tf_op jit(solution)/shard_map/all_gather | solution.py:200
  134.7 1.0 copy-start.3
  135.7 3.4 %copy-start = (bf16[4,2048,512]{2,1,0:T(8,128)(2,1)S(1)}, bf16[4,2048,512]{2,1,0:T(8,128)(2,1)}, u32[]{:S(2)}) copy-start(bf16[4,2048,512]{2,1,0:T(8,128)(2,1)} %constant.66.clone.even_ref) | copy-start | bytes 25165828
  139.1 1.2 copy-start.4
  180.4 2.2 copy-start.1
  182.5 1.6 copy-start.2
  196.7 32.2 %all-to-all-start = ((bf16[32,32,512]{2,1,0:T(8,128)(2,1)}), bf16[32,32,512]{2,1,0:T(8,128)(2,1)S(1)}, u32[]{:S(2)}, u32[]{:S(2)}) async-start(bf16[32,32,512]{2,1,0:T(8,128)(2,1)} %bitcast.6), calls=%async_computation | async-start | bytes 2097152 | tf_op jit(solution)/shard_map/all_to_all | solution.py:202
Sparse Core Ops, SparseCore 0:
  14.0 119.5 all-reduce.2
  150.2 30.1 all-gather.2
